TPU v7x, 128 devices: a whole 4x4x4 slice. The times are simulated.
128 devices in a mesh: band: 4 (over x_lo, core), slab: 32 (over x_hi, z, y).
Axes of the slice: x: 4 (x_hi: 2, x_lo: 2; x = x_hi * 2 + x_lo), y: 4, z: 4, core: 2. Of those that a mesh axis runs over, the one named last changes fastest.
Arguments:
- resident: float32 [8, 128, 128, 128], P('band', 'slab'), may hold values from -5 to 5
- blocks: float32 [16, 128, 128, 128], P('band', 'slab'), may hold values from -5 to 5
- occupation: float32 [16], replicated, may hold values from 0.25 to 1
Outputs:
- exchange_term: float32 [8, 128, 128, 128], P('band', 'slab')
All inputs are finite; a program needn't handle non-finite values.
Results may differ from a plain program's by a relative error of at most 0.0001.
Values sent between devices are 32-bit elements; how exact they have to be, the bound alone decides.
A program may use at most 128 MiB of HBM per device.

v0:
```python
import math
import jax
import jax.numpy as jnp
from jax import lax
from jax.sharding import PartitionSpec as P

KAPPA_SQ = 0.01


def dft_tables(grid_len):
    indices = jnp.arange(grid_len, dtype=jnp.int32)
    product = indices[:, None] * indices[None, :] % grid_len
    angles = product.astype(jnp.float32) * (2.0 * math.pi / grid_len)
    return (jnp.cos(angles), jnp.sin(angles))


def transform(real_part, imag_part, form, cos_t, sin_t, sign_val):

    def apply(values, table):
        return jnp.einsum(
            form, values, table, precision=lax.Precision.HIGHEST, preferred_element_type=jnp.float32
        )

    real_cos = apply(real_part, cos_t)
    real_sin = apply(real_part, sin_t)
    imag_cos = apply(imag_part, cos_t)
    imag_sin = apply(imag_part, sin_t)
    return (real_cos - sign_val * imag_sin, imag_cos + sign_val * real_sin)


def wave_of(indices, grid_len):
    signed = jnp.where(indices > (grid_len - 1) // 2, indices - grid_len, indices)
    return signed.astype(jnp.float32) * (2.0 * math.pi / grid_len)


def coulomb(wave_z, wave_y, wave_x):
    squared = wave_z[:, None, None] ** 2 + wave_y[None, :, None] ** 2 + wave_x[None, None, :] ** 2
    return 4.0 * math.pi / (squared + KAPPA_SQ)


def per_device(resident, blocks, occupation):
    orb_count, plane_count, grid_len, _ = resident.shape
    local_src = blocks.shape[0]
    group_count = lax.axis_size("band")
    src_count = local_src * group_count
    cos_t, sin_t = dft_tables(grid_len)
    along_x = "fzyx,xk->fzyk"
    along_y = "fzyx,yk->fzkx"
    along_z = "fzyx,zk->fkyx"
    source = lax.all_gather(blocks, "band", axis=0, tiled=True)
    count_pairs = source.shape[0] // 2
    even_src = source[0::2]
    odd_src = source[1::2]
    real_part = (resident[:, None] * even_src[None]).reshape(
        orb_count * count_pairs, plane_count, grid_len, grid_len
    )
    imag_part = (resident[:, None] * odd_src[None]).reshape(
        orb_count * count_pairs, plane_count, grid_len, grid_len
    )
    real_part, imag_part = transform(real_part, imag_part, along_x, cos_t, sin_t, -1.0)
    real_part, imag_part = transform(real_part, imag_part, along_y, cos_t, sin_t, -1.0)
    shaped = (orb_count, count_pairs, plane_count, grid_len, grid_len)
    real_part, imag_part = (real_part.reshape(shaped), imag_part.reshape(shaped))
    field_count = orb_count * (src_count // 2)
    flat = (field_count, plane_count, grid_len, grid_len)
    real_part = real_part.reshape(flat)
    imag_part = imag_part.reshape(flat)
    all_waves = wave_of(jnp.arange(grid_len, dtype=jnp.int32), grid_len)
    position = lax.axis_index("slab")
    col_real = lax.all_to_all(real_part, "slab", split_axis=2, concat_axis=1, tiled=True)
    col_imag = lax.all_to_all(imag_part, "slab", split_axis=2, concat_axis=1, tiled=True)
    width_y = col_real.shape[2]
    local_waves = wave_of(position * width_y + jnp.arange(width_y, dtype=jnp.int32), grid_len)
    kernel = coulomb(all_waves, local_waves, all_waves)
    col_real, col_imag = transform(col_real, col_imag, along_z, cos_t, sin_t, -1.0)
    col_real = col_real * kernel[None]
    col_imag = col_imag * kernel[None]
    col_real, col_imag = transform(col_real, col_imag, along_z, cos_t, sin_t, 1.0)
    real_part = lax.all_to_all(col_real, "slab", split_axis=1, concat_axis=2, tiled=True)
    imag_part = lax.all_to_all(col_imag, "slab", split_axis=1, concat_axis=2, tiled=True)
    real_part, imag_part = transform(real_part, imag_part, along_y, cos_t, sin_t, 1.0)
    real_part, imag_part = transform(real_part, imag_part, along_x, cos_t, sin_t, 1.0)
    scale_inv = 1.0 / float(grid_len * grid_len * grid_len)
    shaped = (orb_count, src_count // 2, plane_count, grid_len, grid_len)
    pot_even = real_part.reshape(shaped) * scale_inv
    pot_odd = imag_part.reshape(shaped) * scale_inv
    weighted_even = source[0::2] * occupation[0::2][:, None, None, None]
    weighted_odd = source[1::2] * occupation[1::2][:, None, None, None]
    summed = jnp.sum(pot_even * weighted_even[None], axis=1) + jnp.sum(
        pot_odd * weighted_odd[None], axis=1
    )
    return -summed


def solution(mesh):
    placed = (P("band", "slab", None, None), P("band", "slab", None, None), P())
    return jax.shard_map(
        per_device,
        mesh=mesh,
        in_specs=placed,
        out_specs=P("band", "slab", None, None),
        check_vma=False,
    )
```

profile of v0, /device:TPU:6, one launch (start us, length us, event | category | flops | bytes accessed | tf_op | source)
XLA Modules:
  0.0 448.1 jit_solution(13577813756343298961)
XLA Ops:
  8.8 48.0 %all-gather.2.cloned.1.call-done = f32[16,4,128,128]{3,2,1,0:T(8,128)} async-done(((f32[4,4,128,128]{3,2,1,0:T(8,128)}), f32[16,4,128,128]{3,2,1,0:T(8,128)}) %all-gather.2.cloned.1.call-update) | async-done | bytes 4194320 | tf_op jit(solution)/shard_map/all_gather | solution.py:50
  56.7 4.7 %multiply_multiply_fusion = (f32[8,4,128,128]{3,2,1,0:T(8,128)}, f32[8,4,128,128]{3,2,1,0:T(8,128)S(1)}, f32[8,4,128,128]{3,2,1,0:T(8,128)S(1)}, f32[8,4,128,128]{3,2,1,0:T(8,128)S(1)}) fusion(f32[8]{0:T(128)S(1)} %slice.17, f32[16,4,128,128]{3,2,1,0:T(8,128)} %all-gather.2.cloned.1.call-done, f32[8]{0:T(128)S(1)} %slice.16), kind=kLoop, calls=%fused_computation.30 | loop fusion | flops 2097152 | bytes 12582976 | tf_op jit(solution)/shard_map/mul | solution.py:90
  82.7 15.0 %subtract_bitcast_fusion.1 = f32[16,4,128,128]{3,2,1,0:T(8,128)S(1)} fusion(f32[128,16,4,128]{3,0,2,1:T(8,128)S(1)} %fusion.54, f32[16,4,128,128]{3,2,1,0:T(8,128)S(1)} %multiply_add_fusion), kind=kOutput, calls=%fused_computation.23 | convolution fusion | flops 1612939264 | bytes 12582912 | tf_op jit(solution)/shard_map/fzyx,yk->fzkx/dot_general | solution.py:20
  97.6 4.7 %copy.26 = f32[16,4,128,128]{3,1,0,2:T(4,128)} copy(f32[16,4,128,128]{3,2,1,0:T(8,128)S(1)} %subtract_bitcast_fusion.1) | data formatting | bytes 8388608 | tf_op jit(solution)/shard_map/sub | solution.py:28
  102.3 10.1 %all-to-all-start = ((f32[16,4,128,128]{3,1,0,2:T(4,128)}), f32[16,4,128,128]{3,1,0,2:T(4,128)}, u32[]{:S(2)}, u32[]{:S(2)}) async-start(f32[16,4,128,128]{3,1,0,2:T(4,128)} %copy.26), calls=%async_computation | async-start | bytes 8388608 | tf_op jit(solution)/shard_map/all_to_all | solution.py:70
  112.4 6.1 %fusion.46 = f32[128,16,4,128]{3,0,2,1:T(8,128)S(1)} fusion(f32[16,4,128,128]{3,2,1,0:T(8,128)} %copy-done.2), kind=kOutput, calls=%fused_computation.59 | convolution fusion | flops 1610842112 | bytes 8388608 | tf_op jit(solution)/shard_map/fzyx,yk->fzkx/dot_general | solution.py:20
  122.8 4.7 %copy.31 = f32[16,4,128,128]{3,1,0,2:T(4,128)} copy(f32[16,4,128,128]{3,2,1,0:T(8,128)S(1)} %add_bitcast_fusion.1) | data formatting | bytes 8388608 | tf_op jit(solution)/shard_map/add | solution.py:28
  127.4 43.5 %all-to-all-done = f32[16,4,128,128]{3,1,0,2:T(4,128)} async-done(((f32[16,4,128,128]{3,1,0,2:T(4,128)}), f32[16,4,128,128]{3,1,0,2:T(4,128)}, u32[]{:S(2)}, u32[]{:S(2)}) %all-to-all-start) | async-done | bytes 4194336 | tf_op jit(solution)/shard_map/all_to_all | solution.py:70
  170.9 13.0 %all-to-all-start.1 = ((f32[16,4,128,128]{3,1,0,2:T(4,128)}), f32[16,4,128,128]{3,1,0,2:T(4,128)}, u32[]{:S(2)}, u32[]{:S(2)}) async-start(f32[16,4,128,128]{3,1,0,2:T(4,128)} %copy.31), calls=%async_computation.1 | async-start | bytes 8388608 | tf_op jit(solution)/shard_map/all_to_all | solution.py:71
  184.2 5.3 %copy.27 = f32[16,4,32,4,128]{4,1,2,3,0:T(4,128)} copy(f32[16,4,32,4,128]{4,1,0,3,2:T(4,128)} %bitcast.14) | data formatting | bytes 8388608 | tf_op jit(solution)/shard_map/all_to_all | solution.py:70
  189.5 49.6 %all-to-all-done.1 = f32[16,4,128,128]{3,1,0,2:T(4,128)} async-done(((f32[16,4,128,128]{3,1,0,2:T(4,128)}), f32[16,4,128,128]{3,1,0,2:T(4,128)}, u32[]{:S(2)}, u32[]{:S(2)}) %all-to-all-start.1) | async-done | bytes 4194336 | tf_op jit(solution)/shard_map/all_to_all | solution.py:71
  251.1 5.2 %add_multiply_fusion = f32[128,16,4,128]{3,0,2,1:T(8,128)S(1)} fusion(f32[128,16,4,128]{3,0,2,1:T(8,128)S(1)} %fusion.44, f32[16,128,4,128]{3,1,2,0:T(8,128)S(1)} %bitcast.157, f32[128,4,128]{2,0,1:T(8,128)S(1)} %add_divide_fusion), kind=kOutput, calls=%fused_computation.20 | convolution fusion | flops 1613987840 | bytes 12845056 | tf_op jit(solution)/shard_map/fzyx,zk->fkyx/dot_general | solution.py:20
  256.3 4.8 %subtract_multiply_fusion = f32[128,16,4,128]{3,0,2,1:T(8,128)S(1)} fusion(f32[128,16,4,128]{3,0,2,1:T(8,128)S(1)} %fusion.56, f32[16,128,4,128]{3,1,2,0:T(8,128)S(1)} %bitcast.163, f32[128,4,128]{2,0,1:T(8,128)S(1)} %add_divide_fusion), kind=kOutput, calls=%fused_computation.21 | convolution fusion | flops 1613987840 | bytes 12845056 | tf_op jit(solution)/shard_map/fzyx,zk->fkyx/dot_general | solution.py:20
  265.5 4.8 %subtract_bitcast_fusion = f32[16,128,4,128]{3,1,2,0:T(8,128)S(1)} fusion(f32[128,16,4,128]{3,0,2,1:T(8,128)S(1)} %fusion.10, f32[128,16,4,128]{3,0,2,1:T(8,128)S(1)} %subtract_multiply_fusion), kind=kOutput, calls=%fused_computation.19 | convolution fusion | flops 1611890688 | bytes 12582912 | tf_op jit(solution)/shard_map/fzyx,zk->fkyx/dot_general | solution.py:20
  270.2 4.7 %copy.38 = f32[16,128,4,128]{3,2,0,1:T(4,128)} copy(f32[16,128,4,128]{3,1,2,0:T(8,128)S(1)} %subtract_bitcast_fusion) | data formatting | bytes 8388608 | tf_op jit(solution)/shard_map/sub | solution.py:28
  274.9 8.8 %all-to-all-start.2 = ((f32[16,128,4,128]{3,2,0,1:T(4,128)}), f32[16,128,4,128]{3,2,0,1:T(4,128)}, u32[]{:S(2)}, u32[]{:S(2)}) async-start(f32[16,128,4,128]{3,2,0,1:T(4,128)} %copy.38), calls=%async_computation.2 | async-start | bytes 8388608 | tf_op jit(solution)/shard_map/all_to_all | solution.py:79
  283.7 6.1 %fusion.8 = f32[128,16,4,128]{3,0,2,1:T(8,128)S(1)} fusion(f32[128,16,4,128]{3,0,2,1:T(8,128)} %copy-done.5), kind=kOutput, calls=%fused_computation.8 | convolution fusion | flops 1610842112 | bytes 8388608 | tf_op jit(solution)/shard_map/fzyx,zk->fkyx/dot_general | solution.py:20
  293.8 4.7 %copy.43 = f32[16,128,4,128]{3,2,0,1:T(4,128)} copy(f32[16,128,4,128]{3,1,2,0:T(8,128)S(1)} %add_bitcast_fusion) | data formatting | bytes 8388608 | tf_op jit(solution)/shard_map/add | solution.py:28
  298.5 38.6 %all-to-all-done.2 = f32[16,128,4,128]{3,2,0,1:T(4,128)} async-done(((f32[16,128,4,128]{3,2,0,1:T(4,128)}), f32[16,128,4,128]{3,2,0,1:T(4,128)}, u32[]{:S(2)}, u32[]{:S(2)}) %all-to-all-start.2) | async-done | bytes 4194336 | tf_op jit(solution)/shard_map/all_to_all | solution.py:79
  337.2 7.5 %all-to-all-start.3 = ((f32[16,128,4,128]{3,2,0,1:T(4,128)}), f32[16,128,4,128]{3,2,0,1:T(4,128)}, u32[]{:S(2)}, u32[]{:S(2)}) async-start(f32[16,128,4,128]{3,2,0,1:T(4,128)} %copy.43), calls=%async_computation.3 | async-start | bytes 8388608 | tf_op jit(solution)/shard_map/all_to_all | solution.py:80
  344.7 5.3 %copy.39 = f32[16,32,4,4,128]{4,3,1,2,0:T(4,128)} copy(f32[16,32,4,4,128]{4,3,0,2,1:T(4,128)} %bitcast.32) | data formatting | bytes 8388608 | tf_op jit(solution)/shard_map/all_to_all | solution.py:79
  350.0 52.2 %all-to-all-done.3 = f32[16,128,4,128]{3,2,0,1:T(4,128)} async-done(((f32[16,128,4,128]{3,2,0,1:T(4,128)}), f32[16,128,4,128]{3,2,0,1:T(4,128)}, u32[]{:S(2)}, u32[]{:S(2)}) %all-to-all-start.3) | async-done | bytes 4194336 | tf_op jit(solution)/shard_map/all_to_all | solution.py:80
  414.2 4.6 %convolution_add_fusion = f32[128,16,4,128]{3,0,2,1:T(8,128)S(1)} fusion(f32[128,16,4,128]{3,0,2,1:T(8,128)S(1)} %fusion.41, f32[16,4,128,128]{3,2,1,0:T(8,128)S(1)} %bitcast.159), kind=kOutput, calls=%fused_computation.28 | convolution fusion | flops 1611890688 | bytes 12582912 | tf_op jit(solution)/shard_map/fzyx,yk->fzkx/dot_general | solution.py:20
  426.5 4.7 %convolution_subtract_fusion = f32[128,16,4,128]{3,0,2,1:T(8,128)S(1)} fusion(f32[128,16,4,128]{3,0,2,1:T(8,128)S(1)} %fusion.59, f32[16,4,128,128]{3,2,1,0:T(8,128)S(1)} %bitcast.161), kind=kOutput, calls=%fused_computation.29 | convolution fusion | flops 1611890688 | bytes 12582912 | tf_op jit(solution)/shard_map/fzyx,yk->fzkx/dot_general | solution.py:20
  (48 shorter events, 77.4 us)
Async XLA Ops:
  6.5 50.2 %all-gather.2.cloned.1.call-start = ((), (), s32[]{:S(2)}) async-start(), calls=%async_computation.4 | async-start | bytes 5242880 | tf_op jit(solution)/shard_map/all_gather | solution.py:50
  8.7 52.7 %copy-start.9 = (f32[2,4,128,128]{3,2,1,0:T(8,128)S(1)}, f32[2,4,128,128]{3,2,1,0:T(8,128)}, u32[]{:S(2)}) copy-start(f32[2,4,128,128]{3,2,1,0:T(8,128)} %param.3) | copy-start | bytes 1572868
  74.5 8.2 %copy-start.2 = (f32[16,4,128,128]{3,2,1,0:T(8,128)}, f32[16,4,128,128]{3,2,1,0:T(8,128)S(1)}, u32[]{:S(2)}) copy-start(f32[16,4,128,128]{3,2,1,0:T(8,128)S(1)} %multiply_add_fusion) | copy-start | bytes 12582916
  78.3 4.3 copy-start.3
  102.3 68.6 %all-to-all-start = ((f32[16,4,128,128]{3,1,0,2:T(4,128)}), f32[16,4,128,128]{3,1,0,2:T(4,128)}, u32[]{:S(2)}, u32[]{:S(2)}) async-start(f32[16,4,128,128]{3,1,0,2:T(4,128)} %copy.26), calls=%async_computation | async-start | bytes 8388608 | tf_op jit(solution)/shard_map/all_to_all | solution.py:70
  112.4 6.1 %copy-start.4 = (f32[16,4,128,128]{3,2,1,0:T(8,128)S(1)}, f32[16,4,128,128]{3,2,1,0:T(8,128)}, u32[]{:S(2)}) copy-start(f32[16,4,128,128]{3,2,1,0:T(8,128)} %copy-done.3) | copy-start | bytes 12582916
  170.9 68.2 %all-to-all-start.1 = ((f32[16,4,128,128]{3,1,0,2:T(4,128)}), f32[16,4,128,128]{3,1,0,2:T(4,128)}, u32[]{:S(2)}, u32[]{:S(2)}) async-start(f32[16,4,128,128]{3,1,0,2:T(4,128)} %copy.31), calls=%async_computation.1 | async-start | bytes 8388608 | tf_op jit(solution)/shard_map/all_to_all | solution.py:71
  242.5 4.3 copy-start.6
  256.3 4.8 %copy-start.5 = (f32[128,16,4,128]{3,0,2,1:T(8,128)}, f32[128,16,4,128]{3,0,2,1:T(8,128)S(1)}, u32[]{:S(2)}) copy-start(f32[128,16,4,128]{3,0,2,1:T(8,128)S(1)} %add_multiply_fusion) | copy-start | bytes 12582916
  261.1 4.4 copy-start
  274.9 62.3 %all-to-all-start.2 = ((f32[16,128,4,128]{3,2,0,1:T(4,128)}), f32[16,128,4,128]{3,2,0,1:T(4,128)}, u32[]{:S(2)}, u32[]{:S(2)}) async-start(f32[16,128,4,128]{3,2,0,1:T(4,128)} %copy.38), calls=%async_computation.2 | async-start | bytes 8388608 | tf_op jit(solution)/shard_map/all_to_all | solution.py:79
  283.7 6.1 %copy-start.1 = (f32[128,16,4,128]{3,0,2,1:T(8,128)S(1)}, f32[128,16,4,128]{3,0,2,1:T(8,128)}, u32[]{:S(2)}) copy-start(f32[128,16,4,128]{3,0,2,1:T(8,128)} %copy-done) | copy-start | bytes 12582916
  337.2 65.0 %all-to-all-start.3 = ((f32[16,128,4,128]{3,2,0,1:T(4,128)}), f32[16,128,4,128]{3,2,0,1:T(4,128)}, u32[]{:S(2)}, u32[]{:S(2)}) async-start(f32[16,128,4,128]{3,2,0,1:T(4,128)} %copy.43), calls=%async_computation.3 | async-start | bytes 8388608 | tf_op jit(solution)/shard_map/all_to_all | solution.py:80
  405.6 4.3 copy-start.7
  426.5 4.7 %copy-start.8 = (f32[8,4,128,128]{3,2,1,0:T(8,128)S(1)}, f32[8,4,128,128]{3,2,1,0:T(8,128)}, u32[]{:S(2)}) copy-start(f32[8,4,128,128]{3,2,1,0:T(8,128)} %get-tuple-element.5) | copy-start | bytes 6291460
Sparse Core Ops, SparseCore 0:
  9.0 47.6 all-gather.1
where the time goes:
time: 457 us; the launch traced here: 448 us
  waiting for transfers between devices  233 us (51%)
  matrix products  117 us (26%)
  starting transfers between devices  39.3 us (9%)
  local copies, waits for them, and re-layouts  37.6 us (8%)
  between operations  14.2 us (3%)
  other arithmetic  7.21 us (2%)
    dot_general x24, matrix products, apply(): jnp.einsum(form, values, table, precision=lax.Precision.HIGHEST, preferre...  117 us
    all_to_all x1, waiting for transfers between devices, per_device(): lax.all_to_all(col_imag, 'slab', split_axis=1, concat_axis=2, tiled=True)  52.2 us
    all_to_all x1, waiting for transfers between devices, per_device(): lax.all_to_all(imag_part, 'slab', split_axis=2, concat_axis=1, tiled=True)  49.6 us
    all_gather x1, waiting for transfers between devices, per_device(): source = lax.all_gather(blocks, 'band', axis=0, tiled=True)  48 us
    all_to_all x1, waiting for transfers between devices, per_device(): lax.all_to_all(real_part, 'slab', split_axis=2, concat_axis=1, tiled=True)  43.5 us
    all_to_all x1, waiting for transfers between devices, per_device(): lax.all_to_all(col_real, 'slab', split_axis=1, concat_axis=2, tiled=True)  38.6 us
    all_to_all x1, starting transfers between devices, per_device(): lax.all_to_all(imag_part, 'slab', split_axis=2, concat_axis=1, tiled=True)  13 us
    all_to_all x1, starting transfers between devices, per_device(): lax.all_to_all(real_part, 'slab', split_axis=2, concat_axis=1, tiled=True)  10.1 us
  transfers between devices with their start and end apart: 5, of which 5 were waited for; matrix products, arithmetic and copies ran while one was open for 9% of the time, Pallas kernels for 0%

commit v1 on v0

--- a/solution.py
+++ b/solution.py
@@ -67,7 +67,11 @@
     imag_part = imag_part.reshape(flat)
     all_waves = wave_of(jnp.arange(grid_len, dtype=jnp.int32), grid_len)
     position = lax.axis_index("slab")
-    col_real = lax.all_to_all(real_part, "slab", split_axis=2, concat_axis=1, tiled=True)
+    now = lax.axis_size("slab")
+    reached = jnp.split(real_part, now, axis=2)
+    odd = jnp.stack(reached, axis=0)
+    mat_out = lax.all_to_all(odd, axis_name="slab", split_axis=0, concat_axis=0)
+    col_real = jnp.concatenate(mat_out, 1)
     col_imag = lax.all_to_all(imag_part, "slab", split_axis=2, concat_axis=1, tiled=True)
     width_y = col_real.shape[2]
     local_waves = wave_of(position * width_y + jnp.arange(width_y, dtype=jnp.int32), grid_len)

time: 457 us -> 456 us (level)
  the two profiles are of different devices: /device:TPU:6 before, /device:TPU:16 now
where the time goes in v1:
time: 456 us; the launch traced here: 447 us
  waiting for transfers between devices  219 us (48%)
  matrix products  114 us (25%)
  local copies, waits for them, and re-layouts  53.7 us (12%)
  starting transfers between devices  39.2 us (9%)
  between operations  14.3 us (3%)
  other arithmetic  7.21 us (2%)
    dot_general x24, matrix products, apply(): jnp.einsum(form, values, table, precision=lax.Precision.HIGHEST, preferre...  114 us
    all_to_all x1, waiting for transfers between devices, per_device(): lax.all_to_all(col_imag, 'slab', split_axis=1, concat_axis=2, tiled=True)  50.6 us
    all_gather x1, waiting for transfers between devices, per_device(): source = lax.all_gather(blocks, 'band', axis=0, tiled=True)  48.5 us
    all_to_all x1, waiting for transfers between devices, per_device(): mat_out = lax.all_to_all(odd, axis_name='slab', split_axis=0, concat_axis=0)  42.7 us
    all_to_all x1, waiting for transfers between devices, per_device(): lax.all_to_all(col_real, 'slab', split_axis=1, concat_axis=2, tiled=True)  41 us
    all_to_all x1, waiting for transfers between devices, per_device(): lax.all_to_all(imag_part, 'slab', split_axis=2, concat_axis=1, tiled=True)  35.9 us
    unnamed x53, local copies, waits for them, and re-layouts  21.4 us
    all_to_all x1, starting transfers between devices, per_device(): lax.all_to_all(imag_part, 'slab', split_axis=2, concat_axis=1, tiled=True)  15.4 us
  transfers between devices with their start and end apart: 5, of which 5 were waited for; matrix products, arithmetic and copies ran while one was open for 13% of the time, Pallas kernels for 0%

profile of v1, /device:TPU:16, one launch (start us, length us, event | category | flops | bytes accessed | tf_op | source)
XLA Modules:
  0.0 447.4 jit_solution(2688342162333612199)
XLA Ops:
  8.8 48.5 %all-gather.2.cloned.1.call-done = f32[16,4,128,128]{3,2,1,0:T(8,128)} async-done(((f32[4,4,128,128]{3,2,1,0:T(8,128)}), f32[16,4,128,128]{3,2,1,0:T(8,128)}) %all-gather.2.cloned.1.call-update) | async-done | bytes 4194320 | tf_op jit(solution)/shard_map/all_gather | solution.py:50
  57.2 4.7 %multiply_multiply_fusion = (f32[8,4,128,128]{3,2,1,0:T(8,128)}, f32[8,4,128,128]{3,2,1,0:T(8,128)S(1)}, f32[8,4,128,128]{3,2,1,0:T(8,128)S(1)}, f32[8,4,128,128]{3,2,1,0:T(8,128)S(1)}) fusion(f32[8]{0:T(128)S(1)} %slice.17, f32[16,4,128,128]{3,2,1,0:T(8,128)} %all-gather.2.cloned.1.call-done, f32[8]{0:T(128)S(1)} %slice.16), kind=kLoop, calls=%fused_computation.34 | loop fusion | flops 2097152 | bytes 12582976 | tf_op jit(solution)/shard_map/mul | solution.py:94
  83.1 4.7 %subtract_bitcast_fusion.1 = f32[16,4,128,128]{3,2,1,0:T(8,128)S(1)} fusion(f32[128,16,4,128]{3,0,2,1:T(8,128)S(1)} %fusion.89, f32[16,4,128,128]{3,2,1,0:T(8,128)S(1)} %multiply_add_fusion), kind=kOutput, calls=%fused_computation.23 | convolution fusion | flops 1612939264 | bytes 12582912 | tf_op jit(solution)/shard_map/fzyx,yk->fzkx/dot_general | solution.py:20
  109.9 9.7 %all-to-all-start = ((f32[32,16,4,4,128]{4,3,2,1,0:T(4,128)}), f32[32,16,4,4,128]{4,3,2,1,0:T(4,128)}, u32[]{:S(2)}, u32[]{:S(2)}) async-start(f32[32,16,4,4,128]{4,3,2,1,0:T(4,128)} %fusion.30), calls=%async_computation | async-start | bytes 8388608 | tf_op jit(solution)/shard_map/all_to_all | solution.py:73
  119.6 6.1 %fusion.81 = f32[128,16,4,128]{3,0,2,1:T(8,128)S(1)} fusion(f32[16,4,128,128]{3,2,1,0:T(8,128)} %copy-done.4), kind=kOutput, calls=%fused_computation.126 | convolution fusion | flops 1610842112 | bytes 8388608 | tf_op jit(solution)/shard_map/fzyx,yk->fzkx/dot_general | solution.py:20
  130.0 4.7 %copy.52 = f32[16,4,128,128]{3,1,0,2:T(4,128)} copy(f32[16,4,128,128]{3,2,1,0:T(8,128)S(1)} %add_bitcast_fusion.1) | data formatting | bytes 8388608 | tf_op jit(solution)/shard_map/add | solution.py:28
  134.7 42.7 %all-to-all-done = f32[32,16,4,4,128]{4,3,2,1,0:T(4,128)} async-done(((f32[32,16,4,4,128]{4,3,2,1,0:T(4,128)}), f32[32,16,4,4,128]{4,3,2,1,0:T(4,128)}, u32[]{:S(2)}, u32[]{:S(2)}) %all-to-all-start) | async-done | bytes 4194336 | tf_op jit(solution)/shard_map/all_to_all | solution.py:73
  177.4 15.4 %all-to-all-start.1 = ((f32[16,4,128,128]{3,1,0,2:T(4,128)}), f32[16,4,128,128]{3,1,0,2:T(4,128)}, u32[]{:S(2)}, u32[]{:S(2)}) async-start(f32[16,4,128,128]{3,1,0,2:T(4,128)} %copy.52), calls=%async_computation.1 | async-start | bytes 8388608 | tf_op jit(solution)/shard_map/all_to_all | solution.py:75
  197.0 7.8 %fusion.16 = f32[128,16,4,128]{3,0,2,1:T(8,128)} fusion(f32[16,128,4,128]{3,0,2,1:T(8,128)S(1)} %bitcast.286), kind=kOutput, calls=%fused_computation.26 | convolution fusion | flops 1610842112 | bytes 8388608 | tf_op jit(solution)/shard_map/fzyx,zk->fkyx/dot_general | solution.py:20
  204.7 7.9 %fusion.18 = f32[128,16,4,128]{3,0,2,1:T(8,128)} fusion(f32[16,128,4,128]{3,0,2,1:T(8,128)S(1)} %bitcast.287), kind=kOutput, calls=%fused_computation.28 | convolution fusion | flops 1610842112 | bytes 8388608 | tf_op jit(solution)/shard_map/fzyx,zk->fkyx/dot_general | solution.py:20
  212.6 35.9 %all-to-all-done.1 = f32[16,4,128,128]{3,1,0,2:T(4,128)} async-done(((f32[16,4,128,128]{3,1,0,2:T(4,128)}), f32[16,4,128,128]{3,1,0,2:T(4,128)}, u32[]{:S(2)}, u32[]{:S(2)}) %all-to-all-start.1) | async-done | bytes 4194336 | tf_op jit(solution)/shard_map/all_to_all | solution.py:75
  252.1 5.2 %add_multiply_fusion = f32[128,16,4,128]{3,0,2,1:T(8,128)S(1)} fusion(f32[128,16,4,128]{3,0,2,1:T(8,128)S(1)} %copy-done.8, f32[16,128,4,128]{3,1,2,0:T(8,128)S(1)} %bitcast.280, f32[128,4,128]{2,0,1:T(8,128)S(1)} %add_divide_fusion), kind=kOutput, calls=%fused_computation.20 | convolution fusion | flops 1613987840 | bytes 12845056 | tf_op jit(solution)/shard_map/fzyx,zk->fkyx/dot_general | solution.py:20
  257.2 4.8 %subtract_multiply_fusion = f32[128,16,4,128]{3,0,2,1:T(8,128)S(1)} fusion(f32[128,16,4,128]{3,0,2,1:T(8,128)S(1)} %copy-done.7, f32[16,128,4,128]{3,1,2,0:T(8,128)S(1)} %bitcast.281, f32[128,4,128]{2,0,1:T(8,128)S(1)} %add_divide_fusion), kind=kOutput, calls=%fused_computation.21 | convolution fusion | flops 1613987840 | bytes 12845056 | tf_op jit(solution)/shard_map/fzyx,zk->fkyx/dot_general | solution.py:20
  262.0 4.6 %fusion.10 = f32[128,16,4,128]{3,0,2,1:T(8,128)S(1)} fusion(f32[128,16,4,128]{3,0,2,1:T(8,128)S(1)} %add_multiply_fusion), kind=kOutput, calls=%fused_computation.10 | convolution fusion | flops 1610842112 | bytes 8388608 | tf_op jit(solution)/shard_map/fzyx,zk->fkyx/dot_general | solution.py:20
  271.0 4.7 %copy.60 = f32[16,128,4,128]{3,2,0,1:T(4,128)} copy(f32[16,128,4,128]{3,1,2,0:T(8,128)S(1)} %subtract_bitcast_fusion) | data formatting | bytes 8388608 | tf_op jit(solution)/shard_map/sub | solution.py:28
  275.6 7.4 %all-to-all-start.2 = ((f32[16,128,4,128]{3,2,0,1:T(4,128)}), f32[16,128,4,128]{3,2,0,1:T(4,128)}, u32[]{:S(2)}, u32[]{:S(2)}) async-start(f32[16,128,4,128]{3,2,0,1:T(4,128)} %copy.60), calls=%async_computation.2 | async-start | bytes 8388608 | tf_op jit(solution)/shard_map/all_to_all | solution.py:83
  283.0 6.1 %fusion.8 = f32[128,16,4,128]{3,0,2,1:T(8,128)S(1)} fusion(f32[128,16,4,128]{3,0,2,1:T(8,128)} %copy-done.5), kind=kOutput, calls=%fused_computation.8 | convolution fusion | flops 1610842112 | bytes 8388608 | tf_op jit(solution)/shard_map/fzyx,zk->fkyx/dot_general | solution.py:20
  293.2 4.7 %copy.65 = f32[16,128,4,128]{3,2,0,1:T(4,128)} copy(f32[16,128,4,128]{3,1,2,0:T(8,128)S(1)} %add_bitcast_fusion) | data formatting | bytes 8388608 | tf_op jit(solution)/shard_map/add | solution.py:28
  297.8 41.0 %all-to-all-done.2 = f32[16,128,4,128]{3,2,0,1:T(4,128)} async-done(((f32[16,128,4,128]{3,2,0,1:T(4,128)}), f32[16,128,4,128]{3,2,0,1:T(4,128)}, u32[]{:S(2)}, u32[]{:S(2)}) %all-to-all-start.2) | async-done | bytes 4194336 | tf_op jit(solution)/shard_map/all_to_all | solution.py:83
  338.9 6.7 %all-to-all-start.3 = ((f32[16,128,4,128]{3,2,0,1:T(4,128)}), f32[16,128,4,128]{3,2,0,1:T(4,128)}, u32[]{:S(2)}, u32[]{:S(2)}) async-start(f32[16,128,4,128]{3,2,0,1:T(4,128)} %copy.65), calls=%async_computation.3 | async-start | bytes 8388608 | tf_op jit(solution)/shard_map/all_to_all | solution.py:84
  345.6 5.3 %copy.61 = f32[16,32,4,4,128]{4,3,1,2,0:T(4,128)} copy(f32[16,32,4,4,128]{4,3,0,2,1:T(4,128)} %bitcast.62) | data formatting | bytes 8388608 | tf_op jit(solution)/shard_map/all_to_all | solution.py:83
  350.9 50.6 %all-to-all-done.3 = f32[16,128,4,128]{3,2,0,1:T(4,128)} async-done(((f32[16,128,4,128]{3,2,0,1:T(4,128)}), f32[16,128,4,128]{3,2,0,1:T(4,128)}, u32[]{:S(2)}, u32[]{:S(2)}) %all-to-all-start.3) | async-done | bytes 4194336 | tf_op jit(solution)/shard_map/all_to_all | solution.py:84
  413.5 4.6 %convolution_add_fusion = f32[128,16,4,128]{3,0,2,1:T(8,128)S(1)} fusion(f32[128,16,4,128]{3,0,2,1:T(8,128)S(1)} %fusion.77, f32[16,4,128,128]{3,2,1,0:T(8,128)S(1)} %bitcast.283), kind=kOutput, calls=%fused_computation.32 | convolution fusion | flops 1611890688 | bytes 12582912 | tf_op jit(solution)/shard_map/fzyx,yk->fzkx/dot_general | solution.py:20
  425.7 4.7 %convolution_subtract_fusion = f32[128,16,4,128]{3,0,2,1:T(8,128)S(1)} fusion(f32[128,16,4,128]{3,0,2,1:T(8,128)S(1)} %fusion.93, f32[16,4,128,128]{3,2,1,0:T(8,128)S(1)} %bitcast.285), kind=kOutput, calls=%fused_computation.33 | convolution fusion | flops 1611890688 | bytes 12582912 | tf_op jit(solution)/shard_map/fzyx,yk->fzkx/dot_general | solution.py:20
  (81 shorter events, 94.9 us)
Async XLA Ops:
  6.5 50.7 %all-gather.2.cloned.1.call-start = ((), (), s32[]{:S(2)}) async-start(), calls=%async_computation.4 | async-start | bytes 5242880 | tf_op jit(solution)/shard_map/all_gather | solution.py:50
  8.7 53.2 %copy-start.10 = (f32[2,4,128,128]{3,2,1,0:T(8,128)S(1)}, f32[2,4,128,128]{3,2,1,0:T(8,128)}, u32[]{:S(2)}) copy-start(f32[2,4,128,128]{3,2,1,0:T(8,128)} %param.3) | copy-start | bytes 1572868
  74.9 3.8 copy-start.2
  78.7 4.3 copy-start.4
  109.9 67.5 %all-to-all-start = ((f32[32,16,4,4,128]{4,3,2,1,0:T(4,128)}), f32[32,16,4,4,128]{4,3,2,1,0:T(4,128)}, u32[]{:S(2)}, u32[]{:S(2)}) async-start(f32[32,16,4,4,128]{4,3,2,1,0:T(4,128)} %fusion.30), calls=%async_computation | async-start | bytes 8388608 | tf_op jit(solution)/shard_map/all_to_all | solution.py:73
  119.6 6.1 %copy-start.3 = (f32[16,4,128,128]{3,2,1,0:T(8,128)S(1)}, f32[16,4,128,128]{3,2,1,0:T(8,128)}, u32[]{:S(2)}) copy-start(f32[16,4,128,128]{3,2,1,0:T(8,128)} %copy-done.2) | copy-start | bytes 12582916
  177.4 71.1 %all-to-all-start.1 = ((f32[16,4,128,128]{3,1,0,2:T(4,128)}), f32[16,4,128,128]{3,1,0,2:T(4,128)}, u32[]{:S(2)}, u32[]{:S(2)}) async-start(f32[16,4,128,128]{3,1,0,2:T(4,128)} %copy.52), calls=%async_computation.1 | async-start | bytes 8388608 | tf_op jit(solution)/shard_map/all_to_all | solution.py:75
  248.5 3.5 copy-start.8
  252.0 5.2 %copy-start.7 = (f32[128,16,4,128]{3,0,2,1:T(8,128)S(1)}, f32[128,16,4,128]{3,0,2,1:T(8,128)}, u32[]{:S(2)}) copy-start(f32[128,16,4,128]{3,0,2,1:T(8,128)} %fusion.18) | copy-start | bytes 12582916
  257.2 4.8 %copy-start.5 = (f32[128,16,4,128]{3,0,2,1:T(8,128)}, f32[128,16,4,128]{3,0,2,1:T(8,128)S(1)}, u32[]{:S(2)}) copy-start(f32[128,16,4,128]{3,0,2,1:T(8,128)S(1)} %add_multiply_fusion) | copy-start | bytes 12582916
  262.0 4.6 %copy-start = (f32[128,16,4,128]{3,0,2,1:T(8,128)}, f32[128,16,4,128]{3,0,2,1:T(8,128)S(1)}, u32[]{:S(2)}) copy-start(f32[128,16,4,128]{3,0,2,1:T(8,128)S(1)} %subtract_multiply_fusion) | copy-start | bytes 12582916
  275.6 63.3 %all-to-all-start.2 = ((f32[16,128,4,128]{3,2,0,1:T(4,128)}), f32[16,128,4,128]{3,2,0,1:T(4,128)}, u32[]{:S(2)}, u32[]{:S(2)}) async-start(f32[16,128,4,128]{3,2,0,1:T(4,128)} %copy.60), calls=%async_computation.2 | async-start | bytes 8388608 | tf_op jit(solution)/shard_map/all_to_all | solution.py:83
  283.0 6.1 %copy-start.1 = (f32[128,16,4,128]{3,0,2,1:T(8,128)S(1)}, f32[128,16,4,128]{3,0,2,1:T(8,128)}, u32[]{:S(2)}) copy-start(f32[128,16,4,128]{3,0,2,1:T(8,128)} %copy-done) | copy-start | bytes 12582916
  338.9 62.6 %all-to-all-start.3 = ((f32[16,128,4,128]{3,2,0,1:T(4,128)}), f32[16,128,4,128]{3,2,0,1:T(4,128)}, u32[]{:S(2)}, u32[]{:S(2)}) async-start(f32[16,128,4,128]{3,2,0,1:T(4,128)} %copy.65), calls=%async_computation.3 | async-start | bytes 8388608 | tf_op jit(solution)/shard_map/all_to_all | solution.py:84
  404.8 4.3 copy-start.6
  425.7 4.7 %copy-start.9 = (f32[8,4,128,128]{3,2,1,0:T(8,128)S(1)}, f32[8,4,128,128]{3,2,1,0:T(8,128)}, u32[]{:S(2)}) copy-start(f32[8,4,128,128]{3,2,1,0:T(8,128)} %get-tuple-element.5) | copy-start | bytes 6291460
Sparse Core Ops, SparseCore 0:
  9.0 48.1 all-gather.1
